TPU v7x, 256 devices: a whole 4x4x8 slice. The times are simulated.
256 devices in a mesh: dp: 16 (over z, core), expert: 16 (over x, y).
Axes of the slice: x: 4, y: 4, z: 8, core: 2. Of those that a mesh axis runs over, the one named last changes fastest.
Arguments:
- history: bfloat16 [512, 1024, 2048], P(('dp', 'expert')), may hold values from -6 to 6
- lengths: int32 [512], P(('dp', 'expert')), may hold values from 64 to 1024, as said below
- user_query: bfloat16 [512, 2048], P(('dp', 'expert')), may hold values from -1000 to 1000
- pos_item: bfloat16 [512, 2048], P(('dp', 'expert')), may hold values from -6 to 6
- neg_index: int32 [512, 63], P(('dp', 'expert')), may hold values from 0 to 511
- routes: int32 [32768, 2], P(('dp', 'expert')), may hold values from 0 to 15, all different within a row; in each aligned block of 128 rows (0 to 127, 128 to 255, ...) at most 32 rows name the same one
- w_router: bfloat16 [2048, 16], replicated, may hold values from -0.125 to 0.125
- w_gate: bfloat16 [16, 2048, 768], P('expert', 'dp'), may hold values from -0.125 to 0.125
- w_up: bfloat16 [16, 2048, 768], P('expert', 'dp'), may hold values from -0.125 to 0.125
- w_down: bfloat16 [16, 768, 2048], P('expert', None, 'dp'), may hold values from -0.21875 to 0.21875
- out_gain: float32 [2048], replicated, may hold values from 0.25 to 1.75
Outputs:
- losses: float32 [512], P(('dp', 'expert'))
- grad_gate: float32 [16, 2048, 768], P('expert', 'dp')
- grad_up: float32 [16, 2048, 768], P('expert', 'dp')
- grad_down: float32 [16, 768, 2048], P('expert', None, 'dp')
- grad_router: float32 [2048, 16], replicated
Inputs may be any that keep to these rules, and one draw needn't show every extreme that they name: `lengths`: every device's block of 2 users holds one user with all 1024 events. `neg_index`: indices of users anywhere in the batch. `routes`: each row names two different experts; among the rows of one device no expert is named more than 32 times, a bound that some block reaches.
All inputs are finite; a program needn't handle non-finite values.
Results may differ from a plain program's by a relative error of at most 0.017.
Values may be sent and summed in bfloat16 or wider, within the bound.
A program may use at most 128 MiB of HBM per device.

v0:
```python
import math
import jax
import jax.numpy as jnp
from jax import lax
from jax.sharding import Mesh
from jax.sharding import PartitionSpec as P

D = 2048
HEADS = 16
HEAD = 128
FF = 768
CANDS = 64
EXPERT = ("expert_0", "expert_1")
DP = ("dp_0", "dp_1")
DP_EXPERT = ("dp_0", "dp_1", "expert_0", "expert_1")
norm_eps = 1e-06
loss_scale = 1024.0


def sent_together(arrays, axis, dim, along):
    widths = [a.shape[along] for a in arrays]
    both = jnp.concatenate(arrays, axis=along)
    result = lax.all_gather(both, axis, axis=dim, tiled=True)
    return tuple(jnp.split(result, [sum(widths[:k]) for k in range(1, len(widths))], axis=along))


def whole_of(x, axes, dim):
    result = x
    for number in range(len(axes) - 1, -1, -1):
        result = lax.all_gather(result, axes[number], axis=dim, tiled=True)
    return result


def over_axes_2(x, axes):
    for axis in axes:
        x = lax.psum(x, axis)
    return x


def silu_pair(pre_act):
    sigma_val = jax.nn.sigmoid(pre_act)
    return (pre_act * sigma_val, sigma_val * (1.0 + pre_act * (1.0 - sigma_val)))


def rms_round(values):
    scale_inv = lax.rsqrt(jnp.mean(values * values, axis=-1, keepdims=True) + norm_eps)
    return (values * scale_inv).astype(jnp.bfloat16)


def local(
    history,
    lengths,
    user_query,
    pos_item,
    neg_index,
    routes,
    w_router,
    w_gate,
    w_up,
    w_down,
    out_gain,
):
    user_count = history.shape[0]
    hist_len = history.shape[1]
    model_width = history.shape[2]
    experts = w_router.shape[1]
    expert_devs = lax.axis_size(EXPERT)
    capacity = 4 * user_count * CANDS // experts
    slot_count = expert_devs * capacity
    row_total = user_count * CANDS
    query_heads = user_query.reshape(user_count, HEADS, HEAD)
    key_heads = history.reshape(user_count, hist_len, HEADS, HEAD)
    scores = jnp.einsum(
        "uhd,uthd->uht", query_heads, key_heads, preferred_element_type=jnp.float32
    ) / math.sqrt(HEAD)
    live_mask = jnp.arange(hist_len, dtype=jnp.int32)[None, None, :] < lengths[:, None, None]
    scores = jnp.where(live_mask, scores, -1e30)
    top_val = jnp.max(scores, axis=-1, keepdims=True)
    weights = jnp.where(live_mask, jnp.exp(scores - top_val), 0.0)
    attn_probs = (weights / jnp.sum(weights, axis=-1, keepdims=True)).astype(jnp.bfloat16)
    context = jnp.einsum(
        "uht,uthd->uhd", attn_probs, key_heads, preferred_element_type=jnp.float32
    ).reshape(user_count, model_width)
    all_items = lax.all_gather(pos_item, DP_EXPERT, axis=0, tiled=True)
    candidates = jnp.concatenate([pos_item[:, None, :], all_items[neg_index]], axis=1)
    x_sum = candidates.astype(jnp.float32) + context[:, None, :]
    normed = rms_round(x_sum).reshape(row_total, model_width)
    logits = jnp.dot(normed, w_router, preferred_element_type=jnp.float32)
    affinity = jax.nn.sigmoid(jnp.take_along_axis(logits, routes, axis=1))
    aff_total = jnp.sum(affinity, axis=1, keepdims=True)
    mix = affinity / aff_total
    flat_routes = routes.reshape(-1)
    one_hot = (flat_routes[:, None] == jnp.arange(experts, dtype=jnp.int32)[None, :]).astype(
        jnp.int32
    )
    slot_rank = jnp.sum(jnp.cumsum(one_hot, axis=0) * one_hot, axis=1) - 1
    slot_dest = flat_routes * capacity + slot_rank
    user_base = (lax.axis_index(DP) * expert_devs + lax.axis_index(EXPERT)) * user_count
    own_users = user_base + jnp.arange(user_count, dtype=jnp.int32)
    item_ids = jnp.concatenate([own_users[:, None], neg_index], axis=1).reshape(-1)
    user_ids = (own_users[:, None] + jnp.zeros((user_count, CANDS), jnp.int32)).reshape(-1)
    item_send = (
        jnp.zeros((experts * capacity,), jnp.int32).at[slot_dest].set(jnp.repeat(item_ids, 2))
    )
    user_send = (
        jnp.full((experts * capacity,), -1, jnp.int32).at[slot_dest].set(jnp.repeat(user_ids, 2))
    )
    item_got, user_got = (
        lax.all_to_all(
            item_send.reshape(experts, capacity), EXPERT, split_axis=0, concat_axis=0, tiled=True
        ),
        lax.all_to_all(
            user_send.reshape(experts, capacity), EXPERT, split_axis=0, concat_axis=0, tiled=True
        ),
    )
    group_ctx = lax.all_gather(context, EXPERT, axis=0, tiled=True)
    user_flat = user_got.reshape(-1)
    live_slot = (user_flat >= 0)[:, None]
    local_user = jnp.maximum(user_flat - lax.axis_index(DP) * expert_devs * user_count, 0)
    rebuilt = all_items[item_got.reshape(-1)].astype(jnp.float32) + group_ctx[local_user]
    rows_in = jnp.where(live_slot, rms_round(rebuilt), jnp.zeros((), jnp.bfloat16))
    pieces = sent_together((w_gate[0], w_up[0]), DP, 0, 1)
    columns = rows_in
    gate_pre = jnp.dot(columns, pieces[0], preferred_element_type=jnp.float32)
    up_pre = jnp.dot(columns, pieces[1], preferred_element_type=jnp.float32)
    silu_val, silu_grad = silu_pair(gate_pre)
    hidden = (silu_val * up_pre).astype(jnp.bfloat16)
    expert_out = jnp.dot(
        hidden, whole_of(w_down[0], DP, 1), preferred_element_type=jnp.float32
    ).astype(jnp.bfloat16)
    returned = lax.all_to_all(
        expert_out.reshape(expert_devs, capacity, model_width),
        EXPERT,
        split_axis=0,
        concat_axis=0,
        tiled=True,
    )
    mixed_in = returned.reshape(experts * capacity, model_width)[slot_dest].reshape(
        row_total, 2, model_width
    )
    moe_sum = mix[:, 0:1] * mixed_in[:, 0].astype(jnp.float32) + mix[:, 1:2] * mixed_in[
        :, 1
    ].astype(jnp.float32)
    h_rows = (x_sum.reshape(row_total, model_width) + moe_sum).reshape(
        user_count, CANDS, model_width
    )
    inv_rms = lax.rsqrt(jnp.mean(h_rows * h_rows, axis=-1, keepdims=True) + norm_eps)
    unit_rows = h_rows * inv_rms
    scored = unit_rows * out_gain
    query_f = user_query.astype(jnp.float32)
    listwise = jnp.einsum(
        "ucd,ud->uc", scored, query_f, precision=lax.Precision.HIGHEST
    ) / math.sqrt(D)
    top_list = jnp.max(listwise, axis=-1, keepdims=True)
    expo = jnp.exp(listwise - top_list)
    expo_total = jnp.sum(expo, axis=-1, keepdims=True)
    losses = jnp.log(expo_total[:, 0]) + top_list[:, 0] - listwise[:, 0]
    first_one = (jnp.arange(CANDS, dtype=jnp.int32) == 0).astype(jnp.float32)[None, :]
    d_list = loss_scale * (expo / expo_total - first_one)
    d_scored = d_list[..., None] * query_f[:, None, :] / math.sqrt(D)
    d_unit = d_scored * out_gain
    d_h = inv_rms * (d_unit - unit_rows * jnp.mean(d_unit * unit_rows, axis=-1, keepdims=True))
    d_h = d_h.reshape(row_total, model_width)
    d_out = (mix[:, :, None] * d_h[:, None, :]).astype(jnp.bfloat16)
    d_mix = jnp.sum(d_h[:, None, :] * mixed_in.astype(jnp.float32), axis=-1)
    mix_dot = jnp.sum(mix * d_mix, axis=1, keepdims=True)
    d_aff = (d_mix - mix_dot) / aff_total
    d_pick = d_aff * affinity * (1.0 - affinity)
    route_hot = (routes[:, :, None] == jnp.arange(experts, dtype=jnp.int32)).astype(jnp.float32)
    d_logits = jnp.sum(route_hot * d_pick[:, :, None], axis=1).astype(jnp.bfloat16)
    contract_rows = (((0,), (0,)), ((), ()))
    router_term = lax.dot_general(
        normed, d_logits, contract_rows, preferred_element_type=jnp.float32
    )
    grad_send = (
        jnp.zeros((experts * capacity, model_width), jnp.bfloat16)
        .at[slot_dest]
        .set(d_out.reshape(-1, model_width))
    )
    grad_rows = lax.all_to_all(
        grad_send.reshape(experts, capacity, model_width),
        EXPERT,
        split_axis=0,
        concat_axis=0,
        tiled=True,
    ).reshape(slot_count, model_width)
    contract_cols = (((1,), (1,)), ((), ()))
    columns = grad_rows
    d_hidden = lax.dot_general(
        columns, whole_of(w_down[0], DP, 1), contract_cols, preferred_element_type=jnp.float32
    )
    d_gate = (d_hidden * up_pre * silu_grad).astype(jnp.bfloat16)
    d_up = (d_hidden * silu_val).astype(jnp.bfloat16)
    summed = lax.psum_scatter(
        jnp.concatenate(
            [
                lax.dot_general(rows_in, d_gate, contract_rows, preferred_element_type=jnp.float32),
                lax.dot_general(rows_in, d_up, contract_rows, preferred_element_type=jnp.float32),
                lax.dot_general(
                    grad_rows, hidden, contract_rows, preferred_element_type=jnp.float32
                ),
            ],
            axis=1,
        ).astype(jnp.bfloat16),
        DP,
        scatter_dimension=0,
        tiled=True,
    ).astype(jnp.float32)
    grad_gate = summed[:, :FF][None]
    grad_up = summed[:, FF : 2 * FF][None]
    grad_down = summed[:, 2 * FF :].T[None]
    grad_router = over_axes_2(router_term, DP_EXPERT)
    return (losses, grad_gate, grad_up, grad_down, grad_router)


def solution(mesh):
    torus = Mesh(mesh.devices.reshape(8, 2, 4, 4), ("dp_0", "dp_1", "expert_0", "expert_1"))
    return jax.shard_map(
        local,
        mesh=torus,
        in_specs=(
            P(DP_EXPERT, None, None),
            P(DP_EXPERT),
            P(DP_EXPERT, None),
            P(DP_EXPERT, None),
            P(DP_EXPERT, None),
            P(DP_EXPERT, None),
            P(),
            P(EXPERT, DP, None),
            P(EXPERT, DP, None),
            P(EXPERT, None, DP),
            P(),
        ),
        out_specs=(
            P(DP_EXPERT),
            P(EXPERT, DP, None),
            P(EXPERT, DP, None),
            P(EXPERT, None, DP),
            P(),
        ),
        check_vma=False,
    )
```

profile of v0, /device:TPU:2, one launch (start us, length us, event | category | flops | bytes accessed | tf_op | source)
XLA Modules:
  0.0 581.2 jit_solution(2815404170481698003)
XLA Ops:
  7.2 0.7 all-gather.12.cloned.1.call-update
  8.0 1.8 pad_maximum_fusion.1
  9.8 0.8 copy.92
  12.1 0.7 broadcast_multiply_fusion.2
  13.2 1.4 scatter_custom_fusion
  14.6 0.7 all_to_all.18
  15.3 7.5 %all-to-all-start = ((s32[16,1,32]{2,1,0:T(1,128)}), s32[16,1,32]{2,1,0:T(1,128)S(1)}, u32[]{:S(2)}, u32[]{:S(2)}) async-start(s32[16,1,32]{2,1,0:T(1,128)} %all_to_all.18), calls=%async_computation | async-start | bytes 16384 | tf_op jit(solution)/shard_map/all_to_all | solution.py:112
  22.8 3.7 all-gather
  26.6 5.7 fusion.2
  32.5 5.1 fusion.4
  37.9 23.4 %all-gather.3 = f32[16,2,2048]{2,1,0:T(2,128)S(1)} all-gather(f32[1,2,2048]{2,1,0:T(2,128)S(1)} %reshape.537), channel_id=1, replica_groups=mesh['dp_0'=8,'dp_1'=2,'expert_0'=4,'expert_1'=4] {'expert_0','expert_1'}, dimensions={0}, use_global_device_ids=true | all-gather | bytes 278528 | tf_op jit(solution)/shard_map/all_gather | solution.py:116
  61.7 1.4 scatter_custom_fusion.1
  63.1 0.7 all_to_all.20
  64.2 2.2 mul.310
  66.5 6.3 %all-to-all-start.1 = ((s32[16,1,32]{2,1,0:T(1,128)}), s32[16,1,32]{2,1,0:T(1,128)S(1)}, u32[]{:S(2)}, u32[]{:S(2)}) async-start(s32[16,1,32]{2,1,0:T(1,128)} %all_to_all.20), calls=%async_computation.1 | async-start | bytes 16384 | tf_op jit(solution)/shard_map/all_to_all | solution.py:109
  72.9 5.9 %all-to-all-done.1 = s32[16,1,32]{2,1,0:T(1,128)S(1)} async-done(((s32[16,1,32]{2,1,0:T(1,128)}), s32[16,1,32]{2,1,0:T(1,128)S(1)}, u32[]{:S(2)}, u32[]{:S(2)}) %all-to-all-start.1) | async-done | bytes 2080 | tf_op jit(solution)/shard_map/all_to_all | solution.py:109
  80.2 3.7 gather_fusion.2
  83.8 34.7 %all-gather.12.cloned.1.call-done = bf16[256,2,2048]{2,1,0:T(2,128)(2,1)} async-done(((bf16[1,2,2048]{2,1,0:T(2,128)(2,1)}), bf16[256,2,2048]{2,1,0:T(2,128)(2,1)}) %all-gather.12.cloned.1.call-update) | async-done | bytes 2097168 | tf_op jit(solution)/shard_map/all_gather | solution.py:84
  118.5 2.7 reshape.536
  121.3 3.3 gather_fusion.1
  124.6 3.6 multiply_reduce_fusion
  128.6 0.7 copy-done.3
  129.3 2.0 fusion.19
  131.3 34.9 %all-gather.8.cloned.1.call-done = bf16[2048,1536]{1,0:T(8,128)(2,1)} async-done(((bf16[128,1536]{1,0:T(8,128)(2,1)}), bf16[2048,1536]{1,0:T(8,128)(2,1)}) %all-gather.8.cloned.1.call-update) | async-done | bytes 6291472 | tf_op jit(solution)/shard_map/all_gather | solution.py:23
  166.2 4.5 fusion.10
  170.7 1.1 copy-done.19
  171.9 3.0 multiply_convert_fusion.4
  174.8 46.7 %all-gather.10.cloned.1.call-done = bf16[1,768,2048]{2,1,0:T(8,128)(2,1)} async-done(((bf16[1,768,256]{2,1,0:T(8,128)(2,1)}), bf16[1,768,2048]{2,1,0:T(8,128)(2,1)}) %all-gather.10.cloned.1.call-update) | async-done | bytes 3145744 | tf_op jit(solution)/shard_map/all_gather | solution.py:30
  221.5 5.1 fusion.16
  226.6 7.7 %all-to-all-start.2 = ((bf16[16,32,2048]{2,1,0:T(8,128)(2,1)}), bf16[16,32,2048]{2,1,0:T(8,128)(2,1)}, u32[]{:S(2)}, u32[]{:S(2)}) async-start(bf16[16,32,2048]{2,1,0:T(8,128)(2,1)} %bitcast.109), calls=%async_computation.2 | async-start | bytes 4194304 | tf_op jit(solution)/shard_map/all_to_all | solution.py:131
  234.3 0.9 gather_fusion
  236.6 2.0 gather_fusion.4
  239.3 18.4 %all-to-all-done.2 = bf16[16,32,2048]{2,1,0:T(8,128)(2,1)} async-done(((bf16[16,32,2048]{2,1,0:T(8,128)(2,1)}), bf16[16,32,2048]{2,1,0:T(8,128)(2,1)}, u32[]{:S(2)}, u32[]{:S(2)}) %all-to-all-start.2) | async-done | bytes 2097184 | tf_op jit(solution)/shard_map/all_to_all | solution.py:131
  257.6 4.2 gather_fusion.3
  261.9 0.7 reshape.458
  262.6 2.8 slice_convert_fusion.1
  265.4 3.4 multiply_reduce_fusion.3
  269.0 1.6 copy.111
  270.6 1.7 copy.112
  272.3 1.0 fusion.30
  273.8 2.1 multiply_reduce_fusion.2
  275.9 1.4 subtract_multiply_fusion
  277.7 2.5 mul.322
  280.2 3.8 mul.323
  284.1 4.9 scatter_custom_fusion.2
  288.9 5.9 %all-to-all-start.3 = ((bf16[16,32,2048]{2,1,0:T(8,128)(2,1)}), bf16[16,32,2048]{2,1,0:T(8,128)(2,1)}, u32[]{:S(2)}, u32[]{:S(2)}) async-start(bf16[16,32,2048]{2,1,0:T(8,128)(2,1)} %bitcast.108), calls=%async_computation.3 | async-start | bytes 4194304 | tf_op jit(solution)/shard_map/all_to_all | solution.py:180
  294.9 1.2 multiply_reduce_fusion.1
  296.2 0.8 fusion.73
  297.1 72.1 %all-reduce.5.cloned.1.call-done = f32[2048,16]{0,1:T(8,128)} async-done(((f32[2048,16]{0,1:T(8,128)}), f32[2048,16]{0,1:T(8,128)}) %all-reduce.5.cloned.1.call-update) | async-done | bytes 131088 | tf_op jit(solution)/shard_map/psum | solution.py:36
  369.3 29.7 %all-reduce.7.cloned.1.call-done = f32[2048,16]{0,1:T(8,128)} async-done(((f32[2048,16]{0,1:T(8,128)}), f32[2048,16]{0,1:T(8,128)}) %all-reduce.7.cloned.1.call-update) | async-done | bytes 131088 | tf_op jit(solution)/shard_map/psum | solution.py:36
  399.1 3.8 convolution_convert_fusion
  402.9 3.6 fusion.12
  406.5 1.9 convolution_convert_fusion.1
  408.4 2.1 convolution_convert_fusion.2
  410.5 4.4 pad_maximum_fusion
  414.9 12.2 %copy.109 = bf16[2048,2304]{1,0:T(8,128)(2,1)} copy(bf16[2048,2304]{0,1:T(8,128)(2,1)} %pad_maximum_fusion) | data formatting | bytes 18874368
  427.8 20.0 %all-reduce.9.cloned.1.call-done = f32[2048,16]{0,1:T(8,128)} async-done(((f32[2048,16]{0,1:T(8,128)}), f32[2048,16]{0,1:T(8,128)}) %all-reduce.9.cloned.1.call-update) | async-done | bytes 131088 | tf_op jit(solution)/shard_map/psum | solution.py:36
  447.8 76.7 %reduce-scatter.4.cloned.1.call-done = bf16[128,2304]{1,0:T(8,128)(2,1)} async-done(((bf16[2048,2304]{1,0:T(8,128)(2,1)}), bf16[128,2304]{1,0:T(8,128)(2,1)}) %reduce-scatter.4.cloned.1.call-update) | async-done | bytes 589840
  524.5 1.4 copy.110
  526.0 0.8 slice_bitcast_fusion
  526.8 0.9 copy.100
  527.7 0.9 copy.99
  528.6 43.9 %all-reduce.11.cloned.1.call-done = f32[2048,16]{0,1:T(8,128)} async-done(((f32[2048,16]{0,1:T(8,128)}), f32[2048,16]{0,1:T(8,128)}) %all-reduce.11.cloned.1.call-update) | async-done | bytes 131088 | tf_op jit(solution)/shard_map/psum | solution.py:36
  572.5 1.6 copy.146
  (141 shorter events, 9.4 us)
Async XLA Ops:
  7.2 229.1 %copy-start = (bf16[2048,16]{0,1:T(8,128)(2,1)S(1)}, bf16[2048,16]{0,1:T(8,128)(2,1)}, u32[]{:S(2)}) copy-start(bf16[2048,16]{0,1:T(8,128)(2,1)} %param.17) | copy-start | bytes 196612
  7.2 19.3 %copy-start.16 = (s32[2]{0:T(128)S(1)}, s32[2]{0:T(128)}, u32[]{:S(2)}) copy-start(s32[2]{0:T(128)} %param.12) | copy-start | bytes 28
  7.2 19.4 %copy-start.11 = (bf16[2,2048]{1,0:T(2,128)(2,1)S(1)}, bf16[2,2048]{1,0:T(2,128)(2,1)}, u32[]{:S(2)}) copy-start(bf16[2,2048]{1,0:T(2,128)(2,1)} %param.13) | copy-start | bytes 24580
  7.2 111.3 %all-gather.12.cloned.1.call-start = ((), (), s32[]{:S(2)}) async-start(), calls=%async_computation.11 | async-start | bytes 2105344 | tf_op jit(solution)/shard_map/all_gather | solution.py:84
  7.9 158.3 %all-gather.8.cloned.1.call-start = ((), (), s32[]{:S(2)}) async-start(), calls=%async_computation.5 | async-start | bytes 6684672 | tf_op jit(solution)/shard_map/all_gather | solution.py:23
  15.3 51.2 %all-to-all-start = ((s32[16,1,32]{2,1,0:T(1,128)}), s32[16,1,32]{2,1,0:T(1,128)S(1)}, u32[]{:S(2)}, u32[]{:S(2)}) async-start(s32[16,1,32]{2,1,0:T(1,128)} %all_to_all.18), calls=%async_computation | async-start | bytes 16384 | tf_op jit(solution)/shard_map/all_to_all | solution.py:112
  22.7 198.8 %all-gather.10.cloned.1.call-start = ((), (), s32[]{:S(2)}) async-start(), calls=%async_computation.10 | async-start | bytes 3538944 | tf_op jit(solution)/shard_map/all_gather | solution.py:30
  32.5 5.1 copy-start.15
  32.5 5.3 copy-start.13
  32.5 31.3 %copy-start.12 = (bf16[2,2048]{1,0:T(2,128)(2,1)S(1)}, bf16[2,2048]{1,0:T(2,128)(2,1)}, u32[]{:S(2)}) copy-start(bf16[2,2048]{1,0:T(2,128)(2,1)} %param.14) | copy-start | bytes 24580
  66.5 12.3 %all-to-all-start.1 = ((s32[16,1,32]{2,1,0:T(1,128)}), s32[16,1,32]{2,1,0:T(1,128)S(1)}, u32[]{:S(2)}, u32[]{:S(2)}) async-start(s32[16,1,32]{2,1,0:T(1,128)} %all_to_all.20), calls=%async_computation.1 | async-start | bytes 16384 | tf_op jit(solution)/shard_map/all_to_all | solution.py:109
  124.6 4.1 copy-start.2
  124.6 4.7 copy-start.3
  166.2 5.6 copy-start.7
  166.2 5.6 copy-start.17
  170.7 1.1 copy-start.19
  174.8 51.7 %copy-start.21 = (bf16[512,768]{1,0:T(8,128)(2,1)}, bf16[512,768]{1,0:T(8,128)(2,1)S(1)}, u32[]{:S(2)}) copy-start(bf16[512,768]{1,0:T(8,128)(2,1)S(1)} %get-tuple-element.59) | copy-start | bytes 2359300
  226.6 7.7 %copy-start.14 = (f32[2048]{0:T(1024)S(1)}, f32[2048]{0:T(1024)}, u32[]{:S(2)}) copy-start(f32[2048]{0:T(1024)} %param.21) | copy-start | bytes 24580
  226.6 31.1 %all-to-all-start.2 = ((bf16[16,32,2048]{2,1,0:T(8,128)(2,1)}), bf16[16,32,2048]{2,1,0:T(8,128)(2,1)}, u32[]{:S(2)}, u32[]{:S(2)}) async-start(bf16[16,32,2048]{2,1,0:T(8,128)(2,1)} %bitcast.109), calls=%async_computation.2 | async-start | bytes 4194304 | tf_op jit(solution)/shard_map/all_to_all | solution.py:131
  235.4 0.8 copy-start.9
  236.3 2.2 copy-start.4
  269.0 3.3 copy-start.10
  270.6 3.2 copy-start.6
  288.9 110.2 %all-to-all-start.3 = ((bf16[16,32,2048]{2,1,0:T(8,128)(2,1)}), bf16[16,32,2048]{2,1,0:T(8,128)(2,1)}, u32[]{:S(2)}, u32[]{:S(2)}) async-start(bf16[16,32,2048]{2,1,0:T(8,128)(2,1)} %bitcast.108), calls=%async_computation.3 | async-start | bytes 4194304 | tf_op jit(solution)/shard_map/all_to_all | solution.py:180
  294.9 1.3 copy-start.5
  294.9 74.4 %all-reduce.5.cloned.1.call-start = ((), (), s32[]{:S(2)}) async-start(), calls=%async_computation.6 | async-start | bytes 262144 | tf_op jit(solution)/shard_map/psum | solution.py:36
  297.1 101.9 %all-reduce.7.cloned.1.call-start = ((), (), s32[]{:S(2)}) async-start(), calls=%async_computation.7 | async-start | bytes 262144 | tf_op jit(solution)/shard_map/psum | solution.py:36
  369.3 78.5 %all-reduce.9.cloned.1.call-start = ((), (), s32[]{:S(2)}) async-start(), calls=%async_computation.8 | async-start | bytes 262144 | tf_op jit(solution)/shard_map/psum | solution.py:36
  399.1 125.4 %reduce-scatter.4.cloned.1.call-start = ((), (), s32[]{:S(2)}) async-start(), calls=%async_computation.12 | async-start | bytes 10027008
  399.1 3.8 copy-start.18
  402.9 3.6 copy-start.8
  402.9 3.6 copy-start.20
  406.5 1.9 copy-start.22
  427.1 145.4 %all-reduce.11.cloned.1.call-start = ((), (), s32[]{:S(2)}) async-start(), calls=%async_computation.9 | async-start | bytes 262144 | tf_op jit(solution)/shard_map/psum | solution.py:36
  525.9 48.2 %copy-start.1 = (bf16[2048,16]{0,1:T(8,128)(2,1)S(1)}, bf16[2048,16]{0,1:T(8,128)(2,1)}, u32[]{:S(2)}) copy-start(bf16[2048,16]{0,1:T(8,128)(2,1)} %param.17) | copy-start | bytes 196612
Sparse Core Ops, SparseCore 0:
  11.8 106.7 all-gather.11
  120.9 45.2 all-gather.7
  168.0 53.5 all-gather.9
  298.3 70.9 all-reduce.4
  371.8 27.1 all-reduce.6
  401.3 46.4 all-reduce.8
  450.3 74.1 reduce-scatter.3
  526.8 45.6 all-reduce.10
where the time goes:
time: 589 us; the launch traced here: 581 us
  waiting for transfers between devices  384 us (65%)
  local copies, waits for them, and re-layouts  59.2 us (10%)
  matrix products  36.6 us (6%)
  other arithmetic  31.9 us (5%)
  starting transfers between devices  27.7 us (5%)
  blocking collectives  27.1 us (5%)
  between operations  15 us (3%)
    psum x4, waiting for transfers between devices, over_axes_2(): x = lax.psum(x, axis)  166 us
    unnamed x9, waiting for transfers between devices  77.5 us
    all_gather x1, waiting for transfers between devices, whole_of(): result = lax.all_gather(result, axes[number], axis=dim, tiled=True)  46.7 us
    all_gather x1, waiting for transfers between devices, sent_together(): result = lax.all_gather(both, axis, axis=dim, tiled=True)  34.9 us
    all_gather x1, waiting for transfers between devices, local(): all_items = lax.all_gather(pos_item, DP_EXPERT, axis=0, tiled=True)  34.7 us
    unnamed x59, local copies, waits for them, and re-layouts  26.9 us
    all_gather x1, blocking collectives, local(): group_ctx = lax.all_gather(context, EXPERT, axis=0, tiled=True)  23.4 us
    all_to_all x1, waiting for transfers between devices, local(): lax.all_to_all(expert_out.reshape(expert_devs, capacity, model_width), EX...  18.4 us
  transfers between devices with their start and end apart: 12, of which 10 were waited for; matrix products, arithmetic and copies ran while one was open for 15% of the time, Pallas kernels for 0%

commit v1 on v0

--- a/solution.py
+++ b/solution.py
@@ -1,3 +1,4 @@
+import functools
 import math
 import jax
 import jax.numpy as jnp
@@ -15,6 +16,15 @@
 DP_EXPERT = ("dp_0", "dp_1", "expert_0", "expert_1")
 norm_eps = 1e-06
 loss_scale = 1024.0
+
+
+def pipes_direct(q_in, mesh_ax):
+    e_next = jnp.stack([q_in for _ in range(lax.axis_size(mesh_ax))], 0)
+    long_array = jnp.concatenate(lax.all_to_all(e_next, mesh_ax, 0, 0), 0)
+    return long_array
+
+
+map_yards = functools.partial(pipes_direct, mesh_ax=DP_EXPERT)
 
 
 def sent_together(arrays, axis, dim, along):
@@ -81,7 +91,7 @@
     context = jnp.einsum(
         "uht,uthd->uhd", attn_probs, key_heads, preferred_element_type=jnp.float32
     ).reshape(user_count, model_width)
-    all_items = lax.all_gather(pos_item, DP_EXPERT, axis=0, tiled=True)
+    all_items = map_yards(pos_item)
     candidates = jnp.concatenate([pos_item[:, None, :], all_items[neg_index]], axis=1)
     x_sum = candidates.astype(jnp.float32) + context[:, None, :]
     normed = rms_round(x_sum).reshape(row_total, model_width)

time: 589 us -> 512 us (0.87)
  waiting for transfers between devices: 384 us -> 284 us
  blocking collectives: 27.1 us -> 37.6 us
  starting transfers between devices: 27.7 us -> 35.2 us
    all_gather x1, waiting for transfers between devices: 46.7 us -> 8.04 us  [whole_of(): result = lax.all_gather(result, axes[number], axis=dim, tiled=True)]
    all_gather x1, waiting for transfers between devices: 34.9 us -> 0.01 us  [sent_together(): result = lax.all_gather(both, axis, axis=dim, tiled=True)]
    all_gather x1 -> x0, waiting for transfers between devices: 34.7 us -> none  [local(): all_items = lax.all_gather(pos_item, DP_EXPERT, axis=0, tiled=True)]
    all_to_all x0 -> x1, blocking collectives: none -> 10.5 us  [local(): lax.all_to_all(item_send.reshape(experts, capacity), EXPERT, split_axis=0...]
    all_to_all x1, starting transfers between devices: 6.26 us -> 12.8 us  [pipes_direct(): long_array = jnp.concatenate(lax.all_to_all(e_next, mesh_ax, 0, 0), 0)]
    unnamed x59 -> x60, local copies, waits for them, and re-layouts: 26.9 us -> 24.2 us
    unnamed x9 -> x8, waiting for transfers between devices: 77.5 us -> 76.7 us
  transfers between devices with their start and end apart: 12 -> 11, of which waited for: 10 -> 9; matrix products, arithmetic and copies ran while one was open for 15% -> 17% of each run, Pallas kernels for 0% -> 0%
where the time goes in v1:
time: 512 us; the launch traced here: 503 us
  waiting for transfers between devices  284 us (55%)
  local copies, waits for them, and re-layouts  61.8 us (12%)
  blocking collectives  37.6 us (7%)
  matrix products  36.7 us (7%)
  starting transfers between devices  35.2 us (7%)
  other arithmetic  32.7 us (6%)
  between operations  15 us (3%)
    psum x4, waiting for transfers between devices, over_axes_2(): x = lax.psum(x, axis)  165 us
    unnamed x8, waiting for transfers between devices  76.7 us
    all_gather x1, blocking collectives, local(): group_ctx = lax.all_gather(context, EXPERT, axis=0, tiled=True)  24.7 us
    unnamed x60, local copies, waits for them, and re-layouts  24.2 us
    all_to_all x1, waiting for transfers between devices, local(): lax.all_to_all(expert_out.reshape(expert_devs, capacity, model_width), EX...  20.1 us
    all_to_all x1, starting transfers between devices, pipes_direct(): long_array = jnp.concatenate(lax.all_to_all(e_next, mesh_ax, 0, 0), 0)  12.8 us
    all_to_all x1, waiting for transfers between devices, pipes_direct(): long_array = jnp.concatenate(lax.all_to_all(e_next, mesh_ax, 0, 0), 0)  10.6 us
    all_to_all x1, blocking collectives, local(): lax.all_to_all(item_send.reshape(experts, capacity), EXPERT, split_axis=0...  10.5 us
  transfers between devices with their start and end apart: 11, of which 9 were waited for; matrix products, arithmetic and copies ran while one was open for 17% of the time, Pallas kernels for 0%

profile of v1, /device:TPU:2, one launch (start us, length us, event | category | flops | bytes accessed | tf_op | source)
XLA Modules:
  0.0 503.3 jit_solution(12296068058131228668)
XLA Ops:
  7.2 1.8 pad_maximum_fusion.1
  9.1 0.8 copy.92
  11.4 0.7 broadcast_multiply_fusion.2
  12.4 1.4 scatter_custom_fusion
  13.8 0.7 all_to_all.22
  14.5 7.5 %all-to-all-start.1 = ((s32[16,1,32]{2,1,0:T(1,128)}), s32[16,1,32]{2,1,0:T(1,128)S(1)}, u32[]{:S(2)}, u32[]{:S(2)}) async-start(s32[16,1,32]{2,1,0:T(1,128)} %all_to_all.22), calls=%async_computation.1 | async-start | bytes 16384 | tf_op jit(solution)/shard_map/all_to_all | solution.py:122
  22.0 0.8 pad_add_fusion
  23.0 1.4 scatter_custom_fusion.1
  24.5 3.5 all-to-all-done.1
  28.1 10.5 %all_to_all.33 = s32[16,1,32]{2,1,0:T(1,128)S(1)} all-to-all(s32[16,1,32]{2,1,0:T(1,128)S(1)} %all_to_all.24), channel_id=1, replica_groups=mesh['dp_0'=8,'dp_1'=2,'expert_0'=4,'expert_1'=4] {'expert_0','expert_1'}, dimensions={0} | all-to-all | bytes 4096 | tf_op jit(solution)/shard_map/all_to_all | solution.py:119
  38.6 3.1 stack.2
  41.7 12.8 %all-to-all-start = ((bf16[256,2,2048]{2,1,0:T(2,128)(2,1)}), bf16[256,2,2048]{2,1,0:T(2,128)(2,1)}, u32[]{:S(2)}, u32[]{:S(2)}) async-start(bf16[256,2,2048]{2,1,0:T(2,128)(2,1)} %stack.2), calls=%async_computation | async-start | bytes 4194304 | tf_op jit(solution)/shard_map/all_to_all | solution.py:23
  54.6 2.4 all-gather
  57.1 5.7 %fusion.2 = f32[2,16,1,1024]{3,2,1,0:T(1,128)S(1)} fusion(bf16[2,16,128,1]{2,3,1,0:T(2,128)(2,1)S(1)} %reshape.551, bf16[2,1024,2048]{2,1,0:T(8,128)(2,1)} %param.11), kind=kOutput, calls=%fused_computation.11 | convolution fusion | flops 8388608 | bytes 8527872 | tf_op jit(solution)/shard_map/uhd,uthd->uht/dot_general | solution.py:83
  63.0 5.1 %fusion.4 = f32[2,16,1,128]{3,2,1,0:T(1,128)S(1)} fusion(bf16[2,16,1024,1]{2,1,0,3:T(8,128)(2,1)S(1)} %fusion.26, bf16[2,1024,2048]{2,1,0:T(8,128)(2,1)} %param.11), kind=kOutput, calls=%fused_computation.13 | convolution fusion | flops 8388608 | bytes 8470528 | tf_op jit(solution)/shard_map/uht,uthd->uhd/dot_general | solution.py:91
  68.1 24.7 %all-gather.2 = f32[16,2,2048]{2,1,0:T(2,128)S(1)} all-gather(f32[1,2,2048]{2,1,0:T(2,128)S(1)} %reshape.541), channel_id=1, replica_groups=mesh['dp_0'=8,'dp_1'=2,'expert_0'=4,'expert_1'=4] {'expert_0','expert_1'}, dimensions={0}, use_global_device_ids=true | all-gather | bytes 278528 | tf_op jit(solution)/shard_map/all_gather | solution.py:126
  93.6 2.3 mul.310
  97.4 3.7 gather_fusion.2
  101.1 10.6 %all-to-all-done = bf16[256,2,2048]{2,1,0:T(2,128)(2,1)} async-done(((bf16[256,2,2048]{2,1,0:T(2,128)(2,1)}), bf16[256,2,2048]{2,1,0:T(2,128)(2,1)}, u32[]{:S(2)}, u32[]{:S(2)}) %all-to-all-start) | async-done | bytes 2097184 | tf_op jit(solution)/shard_map/all_to_all | solution.py:23
  111.7 2.8 reshape.452
  114.5 3.3 gather_fusion.1
  117.8 3.7 multiply_reduce_fusion
  122.0 0.7 copy-done.3
  122.6 2.0 fusion.19
  124.6 4.5 fusion.10
  129.2 1.1 copy-done.20
  130.3 3.0 multiply_convert_fusion.4
  133.3 8.0 %all-gather.8.cloned.1.call-done = bf16[1,768,2048]{2,1,0:T(8,128)(2,1)} async-done(((bf16[1,768,256]{2,1,0:T(8,128)(2,1)}), bf16[1,768,2048]{2,1,0:T(8,128)(2,1)}) %all-gather.8.cloned.1.call-update) | async-done | bytes 3145744 | tf_op jit(solution)/shard_map/all_gather | solution.py:40
  141.4 5.1 %fusion.16 = bf16[512,2048]{1,0:T(8,128)(2,1)} fusion(bf16[512,768]{1,0:T(8,128)(2,1)S(1)} %get-tuple-element.59, bf16[1,768,2048]{2,1,0:T(8,128)(2,1)} %all-gather.8.cloned.1.call-done), kind=kOutput, calls=%fused_computation.31 | convolution fusion | flops 1611661312 | bytes 6029312 | tf_op jit(solution)/shard_map/dot_general | solution.py:138
  146.4 7.7 %all-to-all-start.3 = ((bf16[16,32,2048]{2,1,0:T(8,128)(2,1)}), bf16[16,32,2048]{2,1,0:T(8,128)(2,1)}, u32[]{:S(2)}, u32[]{:S(2)}) async-start(bf16[16,32,2048]{2,1,0:T(8,128)(2,1)} %bitcast.108), calls=%async_computation.3 | async-start | bytes 4194304 | tf_op jit(solution)/shard_map/all_to_all | solution.py:141
  154.2 0.9 gather_fusion
  156.4 2.0 gather_fusion.4
  159.1 20.1 %all-to-all-done.3 = bf16[16,32,2048]{2,1,0:T(8,128)(2,1)} async-done(((bf16[16,32,2048]{2,1,0:T(8,128)(2,1)}), bf16[16,32,2048]{2,1,0:T(8,128)(2,1)}, u32[]{:S(2)}, u32[]{:S(2)}) %all-to-all-start.3) | async-done | bytes 2097184 | tf_op jit(solution)/shard_map/all_to_all | solution.py:141
  179.2 4.2 gather_fusion.3
  183.5 0.7 reshape.464
  184.2 2.8 slice_convert_fusion.1
  187.0 3.4 multiply_reduce_fusion.3
  190.6 1.6 copy.111
  192.2 1.7 copy.112
  193.9 1.0 fusion.30
  195.3 2.1 multiply_reduce_fusion.2
  197.5 1.4 subtract_multiply_fusion
  199.3 2.5 mul.322
  201.8 3.8 mul.323
  205.7 4.9 scatter_custom_fusion.2
  210.5 7.0 %all-to-all-start.4 = ((bf16[16,32,2048]{2,1,0:T(8,128)(2,1)}), bf16[16,32,2048]{2,1,0:T(8,128)(2,1)}, u32[]{:S(2)}, u32[]{:S(2)}) async-start(bf16[16,32,2048]{2,1,0:T(8,128)(2,1)} %bitcast.107), calls=%async_computation.4 | async-start | bytes 4194304 | tf_op jit(solution)/shard_map/all_to_all | solution.py:190
  217.6 1.2 multiply_reduce_fusion.1
  218.9 0.8 fusion.73
  219.8 71.6 %all-reduce.5.cloned.1.call-done = f32[2048,16]{0,1:T(8,128)} async-done(((f32[2048,16]{0,1:T(8,128)}), f32[2048,16]{0,1:T(8,128)}) %all-reduce.5.cloned.1.call-update) | async-done | bytes 131088 | tf_op jit(solution)/shard_map/psum | solution.py:46
  291.5 29.7 %all-reduce.7.cloned.1.call-done = f32[2048,16]{0,1:T(8,128)} async-done(((f32[2048,16]{0,1:T(8,128)}), f32[2048,16]{0,1:T(8,128)}) %all-reduce.7.cloned.1.call-update) | async-done | bytes 131088 | tf_op jit(solution)/shard_map/psum | solution.py:46
  321.3 3.8 convolution_convert_fusion
  325.1 3.6 fusion.12
  328.7 1.9 convolution_convert_fusion.1
  330.6 2.1 convolution_convert_fusion.2
  332.7 4.4 pad_maximum_fusion
  337.1 12.2 %copy.109 = bf16[2048,2304]{1,0:T(8,128)(2,1)} copy(bf16[2048,2304]{0,1:T(8,128)(2,1)} %pad_maximum_fusion) | data formatting | bytes 18874368
  350.0 19.9 %all-reduce.9.cloned.1.call-done = f32[2048,16]{0,1:T(8,128)} async-done(((f32[2048,16]{0,1:T(8,128)}), f32[2048,16]{0,1:T(8,128)}) %all-reduce.9.cloned.1.call-update) | async-done | bytes 131088 | tf_op jit(solution)/shard_map/psum | solution.py:46
  370.0 76.6 %reduce-scatter.4.cloned.1.call-done = bf16[128,2304]{1,0:T(8,128)(2,1)} async-done(((bf16[2048,2304]{1,0:T(8,128)(2,1)}), bf16[128,2304]{1,0:T(8,128)(2,1)}) %reduce-scatter.4.cloned.1.call-update) | async-done | bytes 589840
  446.5 1.4 copy.110
  448.0 0.8 slice_bitcast_fusion
  448.8 0.9 copy.100
  449.7 0.9 copy.99
  450.6 44.0 %all-reduce.11.cloned.1.call-done = f32[2048,16]{0,1:T(8,128)} async-done(((f32[2048,16]{0,1:T(8,128)}), f32[2048,16]{0,1:T(8,128)}) %all-reduce.11.cloned.1.call-update) | async-done | bytes 131088 | tf_op jit(solution)/shard_map/psum | solution.py:46
  494.7 1.6 copy.146
  (142 shorter events, 9.4 us)
Async XLA Ops:
  7.2 149.0 %copy-start = (bf16[2048,16]{0,1:T(8,128)(2,1)S(1)}, bf16[2048,16]{0,1:T(8,128)(2,1)}, u32[]{:S(2)}) copy-start(bf16[2048,16]{0,1:T(8,128)(2,1)} %param.17) | copy-start | bytes 196612
  7.2 117.4 %all-gather.6.cloned.1.call-start = ((), (), s32[]{:S(2)}) async-start(), calls=%async_computation.6 | async-start | bytes 6684672 | tf_op jit(solution)/shard_map/all_gather | solution.py:33
  14.5 13.6 %all-to-all-start.1 = ((s32[16,1,32]{2,1,0:T(1,128)}), s32[16,1,32]{2,1,0:T(1,128)S(1)}, u32[]{:S(2)}, u32[]{:S(2)}) async-start(s32[16,1,32]{2,1,0:T(1,128)} %all_to_all.22), calls=%async_computation.1 | async-start | bytes 16384 | tf_op jit(solution)/shard_map/all_to_all | solution.py:122
  41.7 12.8 %copy-start.11 = (bf16[1,768,128]{2,1,0:T(8,128)(2,1)S(1)}, bf16[1,768,128]{2,1,0:T(8,128)(2,1)}, u32[]{:S(2)}) copy-start(bf16[1,768,128]{2,1,0:T(8,128)(2,1)} %param.20) | copy-start | bytes 589828
  41.7 15.2 %copy-start.13 = (bf16[2,2048]{1,0:T(2,128)(2,1)S(1)}, bf16[2,2048]{1,0:T(2,128)(2,1)}, u32[]{:S(2)}) copy-start(bf16[2,2048]{1,0:T(2,128)(2,1)} %param.13) | copy-start | bytes 24580
  41.7 15.3 %copy-start.17 = (s32[2]{0:T(128)S(1)}, s32[2]{0:T(128)}, u32[]{:S(2)}) copy-start(s32[2]{0:T(128)} %param.12) | copy-start | bytes 28
  41.7 70.0 %all-to-all-start = ((bf16[256,2,2048]{2,1,0:T(2,128)(2,1)}), bf16[256,2,2048]{2,1,0:T(2,128)(2,1)}, u32[]{:S(2)}, u32[]{:S(2)}) async-start(bf16[256,2,2048]{2,1,0:T(2,128)(2,1)} %stack.2), calls=%async_computation | async-start | bytes 4194304 | tf_op jit(solution)/shard_map/all_to_all | solution.py:23
  54.5 86.8 %all-gather.8.cloned.1.call-start = ((), (), s32[]{:S(2)}) async-start(), calls=%async_computation.11 | async-start | bytes 3538944 | tf_op jit(solution)/shard_map/all_gather | solution.py:40
  63.0 30.1 %copy-start.16 = (s32[2,63]{1,0:T(2,128)S(1)}, s32[2,63]{1,0:T(2,128)}, u32[]{:S(2)}) copy-start(s32[2,63]{1,0:T(2,128)} %param.15) | copy-start | bytes 1516
  63.0 30.2 %copy-start.12 = (bf16[2,2048]{1,0:T(2,128)(2,1)S(1)}, bf16[2,2048]{1,0:T(2,128)(2,1)}, u32[]{:S(2)}) copy-start(bf16[2,2048]{1,0:T(2,128)(2,1)} %param.14) | copy-start | bytes 24580
  63.0 30.2 %copy-start.14 = (s32[128,2]{0,1:T(2,128)S(1)}, s32[128,2]{0,1:T(2,128)}, u32[]{:S(2)}) copy-start(s32[128,2]{0,1:T(2,128)} %param.16) | copy-start | bytes 3076
  117.8 4.2 copy-start.2
  117.8 4.9 copy-start.3
  124.6 5.7 %copy-start.7 = (bf16[512,2048]{1,0:T(8,128)(2,1)S(1)}, bf16[512,2048]{1,0:T(8,128)(2,1)}, u32[]{:S(2)}) copy-start(bf16[512,2048]{1,0:T(8,128)(2,1)} %fusion.19) | copy-start | bytes 6291460
  124.6 5.7 %copy-start.18 = (bf16[2048,1536]{1,0:T(8,128)(2,1)S(1)}, bf16[2048,1536]{1,0:T(8,128)(2,1)}, u32[]{:S(2)}) copy-start(bf16[2048,1536]{1,0:T(8,128)(2,1)} %all-gather.6.cloned.1.call-done) | copy-start | bytes 18874372
  129.2 1.1 copy-start.20
  133.3 13.1 %copy-start.22 = (bf16[512,768]{1,0:T(8,128)(2,1)}, bf16[512,768]{1,0:T(8,128)(2,1)S(1)}, u32[]{:S(2)}) copy-start(bf16[512,768]{1,0:T(8,128)(2,1)S(1)} %get-tuple-element.59) | copy-start | bytes 2359300
  146.4 7.7 %copy-start.15 = (f32[2048]{0:T(1024)S(1)}, f32[2048]{0:T(1024)}, u32[]{:S(2)}) copy-start(f32[2048]{0:T(1024)} %param.21) | copy-start | bytes 24580
  146.4 32.8 %all-to-all-start.3 = ((bf16[16,32,2048]{2,1,0:T(8,128)(2,1)}), bf16[16,32,2048]{2,1,0:T(8,128)(2,1)}, u32[]{:S(2)}, u32[]{:S(2)}) async-start(bf16[16,32,2048]{2,1,0:T(8,128)(2,1)} %bitcast.108), calls=%async_computation.3 | async-start | bytes 4194304 | tf_op jit(solution)/shard_map/all_to_all | solution.py:141
  155.2 0.8 copy-start.9
  156.2 2.2 copy-start.4
  190.6 3.3 copy-start.10
  192.2 3.2 copy-start.6
  210.5 110.7 %all-to-all-start.4 = ((bf16[16,32,2048]{2,1,0:T(8,128)(2,1)}), bf16[16,32,2048]{2,1,0:T(8,128)(2,1)}, u32[]{:S(2)}, u32[]{:S(2)}) async-start(bf16[16,32,2048]{2,1,0:T(8,128)(2,1)} %bitcast.107), calls=%async_computation.4 | async-start | bytes 4194304 | tf_op jit(solution)/shard_map/all_to_all | solution.py:190
  217.5 1.3 copy-start.5
  217.5 73.9 %all-reduce.5.cloned.1.call-start = ((), (), s32[]{:S(2)}) async-start(), calls=%async_computation.7 | async-start | bytes 262144 | tf_op jit(solution)/shard_map/psum | solution.py:46
  219.7 101.5 %all-reduce.7.cloned.1.call-start = ((), (), s32[]{:S(2)}) async-start(), calls=%async_computation.8 | async-start | bytes 262144 | tf_op jit(solution)/shard_map/psum | solution.py:46
  291.4 78.5 %all-reduce.9.cloned.1.call-start = ((), (), s32[]{:S(2)}) async-start(), calls=%async_computation.9 | async-start | bytes 262144 | tf_op jit(solution)/shard_map/psum | solution.py:46
  321.2 125.3 %reduce-scatter.4.cloned.1.call-start = ((), (), s32[]{:S(2)}) async-start(), calls=%async_computation.12 | async-start | bytes 10027008
  321.3 3.8 copy-start.19
  325.1 3.6 copy-start.8
  325.1 3.6 copy-start.21
  328.7 1.9 copy-start.23
  349.3 145.4 %all-reduce.11.cloned.1.call-start = ((), (), s32[]{:S(2)}) async-start(), calls=%async_computation.10 | async-start | bytes 262144 | tf_op jit(solution)/shard_map/psum | solution.py:46
  447.9 48.4 %copy-start.1 = (bf16[2048,16]{0,1:T(8,128)(2,1)S(1)}, bf16[2048,16]{0,1:T(8,128)(2,1)}, u32[]{:S(2)}) copy-start(bf16[2048,16]{0,1:T(8,128)(2,1)} %param.17) | copy-start | bytes 196612
Sparse Core Ops, SparseCore 0:
  10.4 57.7 all-gather.5
  70.0 71.3 all-gather.7
  221.2 70.1 all-reduce.4
  294.0 27.1 all-reduce.6
  323.5 46.4 all-reduce.8
  372.4 74.1 reduce-scatter.3
  448.8 45.7 all-reduce.10
